TPU v7x, 128 devices: a whole 4x4x4 slice. The times are simulated.
128 devices in a mesh: cx: 8 (over z, core), cy: 16 (over y, x).
Axes of the slice: x: 4, y: 4, z: 4, core: 2. Of those that a mesh axis runs over, the one named last changes fastest.
Arguments:
- latent: float32 [128, 256, 256], P('cx', 'cy'), may hold values from -6 to 6
- observed: float32 [131072], P(('cx', 'cy')), may hold values from -12 to 12
- sigma: float32 [131072], P(('cx', 'cy')), may hold values from 0.5 to 1.5
- response: bfloat16 [65536, 64, 128], P(('cx', 'cy')), may hold values from -0.375 to 0.375
- offsets: int32 [64, 65536], P(None, ('cx', 'cy')), may hold values from 0 to 254
- fractions: float32 [64, 65536], P(None, ('cx', 'cy')), may hold values from 0 to 1
- tile_group: int32 [65536], P(('cx', 'cy')), may hold values from 0 to 7
- tile_slot: int32 [65536], P(('cx', 'cy')), may hold values from 0 to 511, as said below
- send_index: int32 [128, 128, 4], P(('cx', 'cy')), may hold values from -1 to 255, as said below
Outputs:
- gradient: float32 [128, 256, 256], P('cx', 'cy')
- predicted: float32 [131072], P(('cx', 'cy'))
Inputs may be any that keep to these rules, and one draw needn't show every extreme that they name: `send_index`: entries are local column numbers of the sending device, or -1 for an empty slot; for each sender and receiver the used slots come first, 2 to 4 of them; every sender uses all 4 slots for some receiver, and some receiver gets all 4 slots from every sender. `tile_slot`: tile slot q names slot q % 4 from sender q // 4, a slot that this sender uses for this device.
All inputs are finite; a program needn't handle non-finite values.
Results may differ from a plain program's by a relative error of at most 0.0036.
Values may be sent and summed in bfloat16 or wider, within the bound.
A program may use at most 64 MiB of HBM per device.

v0:
```python
import jax
import jax.numpy as jnp
from jax import lax
from jax.sharding import PartitionSpec as P


def padded(cells, sides, width):
    for axis, dim in sides:
        count = lax.axis_size(axis)
        ends = count - 1
        head = lax.slice_in_dim(cells, 0, width, axis=dim)
        tail = lax.slice_in_dim(cells, cells.shape[dim] - width, cells.shape[dim], axis=dim)
        cells = jnp.concatenate(
            [
                lax.ppermute(tail, axis, [(i, (i + 1) % count) for i in range(ends)]),
                cells,
                lax.ppermute(head, axis, [((i + 1) % count, i) for i in range(ends)]),
            ],
            axis=dim,
        )
    return cells


def kernel_taps():
    shifts = jnp.arange(-16, 17).astype(jnp.float32)
    scaled = jnp.sqrt(jnp.float32(3.0)) * jnp.abs(shifts) / 8.0
    raw_taps = (1.0 + scaled) * jnp.exp(-scaled)
    return 0.8 * raw_taps / jnp.sqrt(jnp.sum(raw_taps * raw_taps))


def taps_over(widened, along, length, kernel):
    summed = kernel[0] * lax.slice_in_dim(widened, 0, length, axis=along)
    for shift_at in range(1, 33):
        summed = summed + kernel[shift_at] * lax.slice_in_dim(
            widened, shift_at, shift_at + length, axis=along
        )
    return summed


def smooth(values, kernel):
    rows_x, rows_y, depth = values.shape
    widened = padded(values, (("cx", 0),), 16)
    values = taps_over(widened, 0, rows_x, kernel)
    widened = padded(values, (("cy", 1),), 16)
    values = taps_over(widened, 1, rows_y, kernel)
    widened = jnp.pad(values, ((0, 0), (0, 0), (16, 16)))
    return taps_over(widened, 2, depth, kernel)


def on_device(
    latent, observed, sigma, response, offsets, fractions, tile_group, tile_slot, send_index
):
    kernel = kernel_taps()
    rows_x, rows_y, depth = latent.shape
    across_x = lax.axis_size("cx")
    across_y = lax.axis_size("cy")
    devices = across_x * across_y
    capacity = send_index.shape[2]
    star_tile = response.shape[2]
    groups = observed.shape[0] // star_tile
    density = jnp.exp(smooth(latent, kernel))
    columns = density.reshape(rows_x * rows_y, depth).astype(jnp.bfloat16)
    send_rows = send_index.reshape(devices, capacity)
    valid = send_rows >= 0
    packed = jnp.where(
        valid[..., None], columns[jnp.maximum(send_rows, 0)], jnp.zeros((), jnp.bfloat16)
    )
    received = lax.all_to_all(packed, ("cx", "cy"), split_axis=0, concat_axis=0, tiled=True)
    received = received.reshape(-1)
    sample_at = tile_slot[None, :] * depth + offsets
    lower = received[sample_at].astype(jnp.float32)
    upper = received[sample_at + 1].astype(jnp.float32)
    samples = ((1.0 - fractions) * lower + fractions * upper).astype(jnp.bfloat16)
    tile_pred = jnp.einsum("tms,mt->ts", response, samples, preferred_element_type=jnp.float32)
    one_hot = (tile_group[:, None] == jnp.arange(groups)[None, :]).astype(jnp.float32)
    predicted = jnp.dot(one_hot.T, tile_pred, precision=lax.Precision.HIGHEST)
    stars_obs = observed.reshape(groups, star_tile)
    stars_sig = sigma.reshape(groups, star_tile)
    resid = (predicted - stars_obs) / (stars_sig * stars_sig)
    tile_resid = jnp.dot(one_hot, resid, precision=lax.Precision.HIGHEST).astype(jnp.bfloat16)
    back = jnp.einsum("tms,ts->mt", response, tile_resid, preferred_element_type=jnp.float32)
    flat_grad = jnp.zeros((devices * capacity * depth,), jnp.float32)
    flat_grad = flat_grad.at[sample_at].add((1.0 - fractions) * back)
    flat_grad = flat_grad.at[sample_at + 1].add(fractions * back)
    returned = lax.all_to_all(
        flat_grad.reshape(devices, capacity, depth).astype(jnp.bfloat16),
        ("cx", "cy"),
        split_axis=0,
        concat_axis=0,
        tiled=True,
    ).astype(jnp.float32)
    returned = returned.reshape(devices * capacity, depth)
    targets = jnp.where(valid, send_rows, rows_x * rows_y).reshape(-1)
    column_grad = jax.ops.segment_sum(returned, targets, num_segments=rows_x * rows_y + 1)[
        : rows_x * rows_y
    ]
    dens_grad = column_grad.reshape(rows_x, rows_y, depth)
    gradient = latent + smooth(density * dens_grad, kernel)
    return (gradient, predicted.reshape(-1))


def solution(mesh):
    placed = (
        P("cx", "cy", None),
        P(("cx", "cy")),
        P(("cx", "cy")),
        P(("cx", "cy"), None, None),
        P(None, ("cx", "cy")),
        P(None, ("cx", "cy")),
        P(("cx", "cy")),
        P(("cx", "cy")),
        P(("cx", "cy"), None, None),
    )
    return jax.shard_map(
        on_device,
        mesh=mesh,
        in_specs=placed,
        out_specs=(P("cx", "cy", None), P(("cx", "cy"))),
        check_vma=False,
    )
```

profile of v0, /device:TPU:1, one launch (start us, length us, event | category | flops | bytes accessed | tf_op | source)
XLA Modules:
  0.0 988.9 jit_solution(6181617344309543160)
XLA Ops:
  0.6 4.9 collective-permute-start
  14.0 22.2 %fusion.402 = f32[16,16,256]{2,1,0:T(8,128)S(1)} fusion(f32[32,16,256]{2,1,0:T(8,128)S(1)} %constant_dynamic-update-slice_fusion.2, f32[32,16,256]{2,1,0:T(8,128)S(1)} %get-tuple-element.6, f32[16,16,256]{2,1,0:T(8,128)S(1)} %collective-permute-done.1, f32[16,16,256]{2,1,0:T(8,128)} %param.9, f32[16,16,256]{2,1,0:T(8,128)S(1)} %collective-permute-done, ...), kind=kLoop, calls=%fused_computation.650 | loop fusion | flops 4259840 | bytes 8913028 | tf_op jit(solution)/shard_map/add | solution.py:34
  37.5 4.0 collective-permute-start.2
  41.7 2.1 collective-permute-done.3
  45.5 22.1 %fusion.311 = f32[16,16,256]{2,1,0:T(8,128)S(1)} fusion(f32[16,16,256]{2,1,0:T(8,128)S(1)} %fusion.402, f32[16,16,256]{2,1,0:T(8,128)S(1)} %collective-permute-done.3, f32[16,16,256]{2,1,0:T(8,128)S(1)} %collective-permute-done.2, f32[]{:T(128)} %bitcast.32, f32[]{:T(128)} %bitcast.31, f32[]{:T(128)} %bitcast.30, f32[]{:T(128)} %bitcast.29, f32[]{:T(128)} %bitcast.28, ...), kind=kLoop, calls=%fused_computation.552 | loop fusion | flops 6225920 | bytes 1048708 | tf_op jit(solution)/shard_map/add | solution.py:34
  67.6 22.8 %fusion.448 = (bf16[16,16,256]{2,1,0:T(8,128)(2,1)S(1)}, f32[16,16,256]{2,1,0:T(8,128)S(1)}) fusion(f32[]{:T(128)} %bitcast.32, f32[]{:T(128)} %bitcast.31, f32[]{:T(128)} %bitcast.30, f32[]{:T(128)} %bitcast.29, f32[]{:T(128)} %bitcast.28, f32[]{:T(128)} %bitcast.27, f32[]{:T(128)} %bitcast.26, f32[]{:T(128)} %bitcast.25, f32[]{:T(128)} %bitcast.24, ...), kind=kLoop, calls=%fused_computation.746 | loop fusion | flops 4325376 | bytes 655492 | tf_op jit(solution)/shard_map/convert_element_type | solution.py:62
  93.4 14.9 %all-to-all-start = ((bf16[128,4,256]{2,1,0:T(4,128)(2,1)}), bf16[128,4,256]{2,1,0:T(4,128)(2,1)S(1)}, u32[]{:S(2)}, u32[]{:S(2)}) async-start(bf16[128,4,256]{2,1,0:T(4,128)(2,1)} %broadcast_select_fusion), calls=%async_computation | async-start | bytes 524288 | tf_op jit(solution)/shard_map/all_to_all | solution.py:68
  108.4 11.2 %all-to-all-done = bf16[128,4,256]{2,1,0:T(4,128)(2,1)S(1)} async-done(((bf16[128,4,256]{2,1,0:T(4,128)(2,1)}), bf16[128,4,256]{2,1,0:T(4,128)(2,1)S(1)}, u32[]{:S(2)}, u32[]{:S(2)}) %all-to-all-start) | async-done | bytes 262176 | tf_op jit(solution)/shard_map/all_to_all | solution.py:68
  119.8 201.3 %gather_fusion.2 = bf16[32768]{0:T(1024)(128)(2,1)S(1)} fusion(bf16[131072]{0:T(1024)(128)(2,1)S(1)} %bitcast.80, s32[32768]{0:T(1024)S(1)} %broadcast_clamp_fusion), kind=kCustom, calls=%fused_computation.2 | custom fusion | bytes 262144 | tf_op jit(solution)/shard_map/gather | solution.py:72
  321.2 201.3 %gather_fusion.1 = bf16[32768]{0:T(1024)(128)(2,1)S(1)} fusion(bf16[131072]{0:T(1024)(128)(2,1)S(1)} %bitcast.81, s32[32768]{0:T(1024)S(1)} %broadcast_clamp_fusion.1), kind=kCustom, calls=%fused_computation.1 | custom fusion | bytes 262144 | tf_op jit(solution)/shard_map/gather | solution.py:71
  522.8 5.7 fusion.452
  529.3 7.8 fusion.433
  537.3 171.2 %scatter_custom_fusion = f32[131072]{0:T(1024)S(1)} fusion(s32[32768]{0:T(1024)S(1)} %bitcast.89, f32[32768]{0:T(1024)S(1)} %bitcast.91, f32[]{:T(128)} %constant.15.clone.1), kind=kCustom, calls=%fused_computation.714 | custom fusion | flops 32768 | bytes 524292 | tf_op jit(solution)/shard_map/scatter-add | solution.py:83
  708.5 175.2 %scatter_fusion = f32[131072]{0:T(1024)S(1)} fusion(f32[131072]{0:T(1024)S(1)} %scatter_custom_fusion, s32[32768]{0:T(1024)S(1)} %bitcast.84, f32[32768]{0:T(1024)S(1)} %bitcast.87), kind=kCustom, calls=%fused_computation.4 | custom fusion | flops 32768 | bytes 524288 | tf_op jit(solution)/shard_map/scatter-add | solution.py:84
  884.7 4.2 all-to-all-start.1
  889.1 11.1 %all-to-all-done.1 = bf16[128,4,256]{2,1,0:T(4,128)(2,1)S(1)} async-done(((bf16[128,4,256]{2,1,0:T(4,128)(2,1)}), bf16[128,4,256]{2,1,0:T(4,128)(2,1)S(1)}, u32[]{:S(2)}, u32[]{:S(2)}) %all-to-all-start.1) | async-done | bytes 262176 | tf_op jit(solution)/shard_map/all_to_all | solution.py:85
  900.2 3.3 scatter_custom_fusion.2
  903.7 2.6 collective-permute-start.5
  906.3 3.2 collective-permute-start.4
  912.5 21.2 %fusion.223 = f32[16,16,256]{2,1,0:T(8,128)S(1)} fusion(f32[16,16,256]{2,1,0:T(8,128)S(1)} %mul.1046, f32[16,16,256]{2,1,0:T(8,128)S(1)} %collective-permute-done.5, f32[16,16,256]{2,1,0:T(8,128)S(1)} %collective-permute-done.4, f32[]{:T(128)} %bitcast.32, f32[]{:T(128)} %bitcast.31, f32[]{:T(128)} %bitcast.30, f32[]{:T(128)} %bitcast.29, f32[]{:T(128)} %bitcast.28, ...), kind=kLoop, calls=%fused_computation.464 | loop fusion | flops 6225920 | bytes 1048708 | tf_op jit(solution)/shard_map/add | solution.py:34
  935.1 4.0 collective-permute-start.6
  939.1 2.4 collective-permute-done.7
  943.2 22.1 %fusion.135 = f32[16,16,256]{2,1,0:T(8,128)S(1)} fusion(f32[16,16,256]{2,1,0:T(8,128)S(1)} %fusion.223, f32[16,16,256]{2,1,0:T(8,128)S(1)} %collective-permute-done.7, f32[16,16,256]{2,1,0:T(8,128)S(1)} %collective-permute-done.6, f32[]{:T(128)} %bitcast.32, f32[]{:T(128)} %bitcast.31, f32[]{:T(128)} %bitcast.30, f32[]{:T(128)} %bitcast.29, f32[]{:T(128)} %bitcast.28, ...), kind=kLoop, calls=%fused_computation.376 | loop fusion | flops 6225920 | bytes 1048708 | tf_op jit(solution)/shard_map/add | solution.py:34
  965.3 23.6 %fusion.121 = f32[16,16,256]{2,1,0:T(8,128)} fusion(f32[16,16,256]{2,1,0:T(8,128)S(1)} %copy-done, f32[16,16,256]{2,1,0:T(8,128)S(1)} %fusion.135, f32[]{:T(128)} %bitcast.32, f32[]{:T(128)} %bitcast.31, f32[]{:T(128)} %bitcast.30, f32[]{:T(128)} %bitcast.29, f32[]{:T(128)} %bitcast.28, f32[]{:T(128)} %bitcast.27, f32[]{:T(128)} %bitcast.26, f32[]{:T(128)} %bitcast.25, ...), kind=kLoop, calls=%fused_computation.362 | loop fusion | flops 4325376 | bytes 786564 | tf_op jit(solution)/shard_map/add | solution.py:98
  (64 shorter events, 22.7 us)
Async XLA Ops:
  0.6 40.9 %copy-start.2 = (s32[1,128,4]{1,2,0:T(4,128)S(1)}, s32[1,128,4]{1,2,0:T(4,128)}, u32[]{:S(2)}) copy-start(s32[1,128,4]{1,2,0:T(4,128)} %param.17) | copy-start | bytes 6148
  0.6 12.3 %collective-permute-start = (f32[16,16,256]{2,1,0:T(8,128)}, f32[16,16,256]{2,1,0:T(8,128)S(1)}, u32[]{:S(2)}, u32[]{:S(2)}) collective-permute-start(f32[16,16,256]{2,1,0:T(8,128)} %param.9), channel_id=1, source_target_pairs={{0,16},{16,32},{32,48},{48,64},{64,80},{80,96},{96,112},{1,17},{17... | collective-permute-start | bytes 786440 | tf_op jit(solution)/shard_map/ppermute | solution.py:15
  5.6 8.4 collective-permute-start.1
  36.2 7.5 collective-permute-start.3
  37.5 8.0 collective-permute-start.2
  93.4 26.2 %all-to-all-start = ((bf16[128,4,256]{2,1,0:T(4,128)(2,1)}), bf16[128,4,256]{2,1,0:T(4,128)(2,1)S(1)}, u32[]{:S(2)}, u32[]{:S(2)}) async-start(bf16[128,4,256]{2,1,0:T(4,128)(2,1)} %broadcast_select_fusion), calls=%async_computation | async-start | bytes 524288 | tf_op jit(solution)/shard_map/all_to_all | solution.py:68
  321.2 201.4 %copy-start.1 = (f32[64,512]{1,0:T(8,128)S(1)}, f32[64,512]{1,0:T(8,128)}, u32[]{:S(2)}) copy-start(f32[64,512]{1,0:T(8,128)} %param.14) | copy-start | bytes 393220
  522.7 5.7 copy-start.4
  522.8 6.2 copy-start.5
  522.8 6.2 copy-start.6
  528.9 354.8 %copy-start.3 = (f32[8,128]{1,0:T(8,128)}, f32[8,128]{1,0:T(8,128)S(1)}, u32[]{:S(2)}) copy-start(f32[8,128]{1,0:T(8,128)S(1)} %fusion.435) | copy-start | bytes 12292
  708.5 256.8 %copy-start = (f32[16,16,256]{2,1,0:T(8,128)S(1)}, f32[16,16,256]{2,1,0:T(8,128)}, u32[]{:S(2)}) copy-start(f32[16,16,256]{2,1,0:T(8,128)} %param.9) | copy-start | bytes 786436
  884.7 15.5 %all-to-all-start.1 = ((bf16[128,4,256]{2,1,0:T(4,128)(2,1)}), bf16[128,4,256]{2,1,0:T(4,128)(2,1)S(1)}, u32[]{:S(2)}, u32[]{:S(2)}) async-start(bf16[128,4,256]{2,1,0:T(4,128)(2,1)} %convert_element_type.42), calls=%async_computation.1 | async-start | bytes 524288 | tf_op jit(solution)/shard_map/all_to_all | solution.py:85
  903.7 7.7 collective-permute-start.5
  906.3 6.3 collective-permute-start.4
  933.8 7.7 collective-permute-start.7
  935.1 8.1 collective-permute-start.6
where the time goes:
time: 995 us; the launch traced here: 989 us
  other arithmetic  488 us (49%)
  local copies, waits for them, and re-layouts  409 us (41%)
  starting transfers between devices  42.3 us (4%)
  waiting for transfers between devices  33.3 us (3%)
  matrix products  14.2 us (1%)
    gather x1, local copies, waits for them, and re-layouts, on_device(): lower = received[sample_at].astype(jnp.float32)  201 us
    gather x1, local copies, waits for them, and re-layouts, on_device(): upper = received[sample_at + 1].astype(jnp.float32)  201 us
    scatter-add x1, other arithmetic, on_device(): flat_grad = flat_grad.at[sample_at + 1].add(fractions * back)  175 us
    scatter-add x1, other arithmetic, on_device(): flat_grad = flat_grad.at[sample_at].add((1.0 - fractions) * back)  171 us
    add x4, other arithmetic, taps_over(): summed + kernel[shift_at] * lax.slice_in_dim(widened, shift_at, shift_at...  87.6 us
    add x1, other arithmetic, on_device(): gradient = latent + smooth(density * dens_grad, kernel)  23.6 us
    convert_element_type x1, other arithmetic, on_device(): columns = density.reshape(rows_x * rows_y, depth).astype(jnp.bfloat16)  22.8 us
  transfers between devices with their start and end apart: 10, of which 8 were waited for; matrix products, arithmetic and copies ran while one was open for 1% of the time, Pallas kernels for 0%

commit v1 on v0

v1 whole, which is shorter than its diff:
```python
import functools

import jax
import jax.numpy as jnp
import ml_dtypes
import numpy as np
from jax import lax
from jax.experimental import pallas as pl
from jax.experimental.pallas import tpu as pltpu
from jax.sharding import PartitionSpec as P

F32, BF16 = jnp.float32, jnp.bfloat16
MESH = pl.DeviceIdType.MESH
LANES = 128


def smoothing_tables(rows_x, rows_y, depth):
    shifts = np.arange(-16, 17).astype(np.float32)
    scaled = np.sqrt(np.float32(3.0)) * np.abs(shifts) / np.float32(8.0)
    raw = (np.float32(1.0) + scaled) * np.exp(-scaled)
    taps = np.float32(0.8) * raw / np.sqrt(np.sum(raw * raw))

    def band(length, start):
        shift = np.arange(length)[None, :] + start - np.arange(length)[:, None]
        inside = np.abs(shift) <= 16
        return np.where(inside, taps[np.clip(shift + 16, 0, 32)], 0).astype(np.float32)

    whole = [np.kron(band(rows_x, s), np.eye(rows_y)) for s in (0, -rows_x, rows_x)]
    whole += [np.kron(np.eye(rows_x), band(rows_y, s)) for s in (0, -rows_y, rows_y)]
    whole += [band(depth, 0)]
    parts = []
    for table in whole:
        table = table.astype(np.float32)
        high = table.astype(ml_dtypes.bfloat16)
        parts += [high, (table - high.astype(np.float32)).astype(ml_dtypes.bfloat16)]
    return np.stack(parts)


def dot(a, b):
    return lax.dot_general(a, b, (((1,), (0,)), ((), ())), preferred_element_type=F32)


def dot_t(a, b):
    return lax.dot_general(a, b, (((1,), (1,)), ((), ())), preferred_element_type=F32)


def split(x):
    high = x.astype(BF16)
    return high, (x - high.astype(F32)).astype(BF16)


def one_hot(a, b):
    return jnp.where(a == b, 1.0, 0.0).astype(BF16)


def kernel(
    ncx, ncy, cap,
    latent, observed, sigma, response, offsets, fractions, group, slot, send, tables,
    gradient, predicted,
    resp, tabs, halo_out, halo_in, a_out, a_in, b_out, b_in, c_out, c_in, d_out, d_in,
    index, weight, odup, block_of, tile_pred, tile_resid, tile_grad, hot_out, hot_back,
    hot_slot, density,
    resp_sem, tab_sem, halo_send, halo_recv, x_send, x_recv, y_send, y_recv,
):
    cx, cy = lax.axis_index("cx"), lax.axis_index("cy")
    tiles = slot.shape[1]
    slots = ncx * ncy * cap
    samples = offsets.shape[0]
    chunk_rows = resp.shape[0] // resp_sem.shape[0]

    tab_copy = pltpu.make_async_copy(tables, tabs, tab_sem)
    tab_copy.start()
    resp_copies = [
        pltpu.make_async_copy(
            response.at[pl.ds(i * chunk_rows, chunk_rows)],
            resp.at[pl.ds(i * chunk_rows, chunk_rows)],
            resp_sem.at[i],
        )
        for i in range(resp_sem.shape[0])
    ]
    for copy in resp_copies:
        copy.start()

    barrier = pltpu.get_barrier_semaphore()
    for k in range(1, ncx):
        pl.semaphore_signal(
            barrier, inc=1, device_id=(lax.rem(cx + k, ncx), cy), device_id_type=MESH
        )
    for k in range(1, ncy):
        pl.semaphore_signal(
            barrier, inc=1, device_id=(cx, lax.rem(cy + k, ncy)), device_id_type=MESH
        )
    halo_out[0] = latent[...].astype(BF16)
    pl.semaphore_wait(barrier, ncx + ncy - 2)

    def start_halo(at, along):
        copies = []
        for side in range(2):
            step = 1 if side == 0 else -1
            if along == "x":
                to = (lax.rem(cx + step + ncx, ncx), cy)
            else:
                to = (cx, lax.rem(cy + step + ncy, ncy))
            copy = pltpu.make_async_remote_copy(
                src_ref=halo_out.at[at],
                dst_ref=halo_in.at[2 * at + side],
                send_sem=halo_send.at[2 * at + side],
                recv_sem=halo_recv.at[2 * at + side],
                device_id=to,
                device_id_type=MESH,
            )
            copy.start()
            copies.append(copy)
        return copies

    def own_part(x, at):
        high, low = split(x)
        return (
            dot(tabs[2 * at], high) + dot(tabs[2 * at + 1], high) + dot(tabs[2 * at], low)
        )

    def halo_part(copies, at, first):
        place, count = (cx, ncx) if first == 0 else (cy, ncy)
        copies[0].wait_recv()
        copies[1].wait_recv()
        left = halo_in[2 * at]
        right = halo_in[2 * at + 1]
        from_left = dot(tabs[2 * first + 2], left) + dot(tabs[2 * first + 3], left)
        from_right = dot(tabs[2 * first + 4], right) + dot(tabs[2 * first + 5], right)
        zero = jnp.zeros_like(from_left)
        return jnp.where(place > 0, from_left, zero) + jnp.where(
            place < count - 1, from_right, zero
        )

    def along_z(x):
        high, low = split(x)
        return dot(high, tabs[12]) + dot(high, tabs[13]) + dot(low, tabs[12])

    def swap(out, into, along):
        count, me = (ncx, cx) if along == "x" else (ncy, cy)
        send_sem, recv_sem = (x_send, x_recv) if along == "x" else (y_send, y_recv)
        at = 0 if (into is a_in or into is b_in) else 1
        copies = []
        for k in range(1, count):
            to = lax.rem(me + k, count)
            copy = pltpu.make_async_remote_copy(
                src_ref=out.at[to],
                dst_ref=into.at[me],
                send_sem=send_sem.at[at * count + k],
                recv_sem=recv_sem.at[at * count + k],
                device_id=(to, cy) if along == "x" else (cx, to),
                device_id_type=MESH,
            )
            copy.start()
            copies.append(copy)
        into[me] = out[me]
        return copies

    started = []
    copies = start_halo(0, "x")
    started += copies

    def columns_of(row):
        return jnp.broadcast_to(row.astype(F32), (LANES, row.shape[1])).T

    lane_of = lax.broadcasted_iota(jnp.int32, (1, LANES), 1).astype(F32)
    voxels = latent.shape[0]
    depth = latent.shape[1]
    send_col = columns_of(send[...])
    for j in range(voxels // LANES):
        hot_out[:, j * LANES : (j + 1) * LANES] = one_hot(send_col, lane_of + j * LANES)
    row_of = lax.broadcasted_iota(jnp.int32, (voxels, 1), 0).astype(F32)
    hot_back[...] = one_hot(row_of, send[...].astype(F32))
    q = slot[...]
    per_x = ncy * cap
    place = (lax.rem(q, per_x) // cap) * (ncx * cap) + (q // per_x) * cap + lax.rem(q, cap)
    place_row = place.astype(F32)
    slot_row = lax.broadcasted_iota(jnp.int32, (slots, 1), 0).astype(F32)
    hot_slot[...] = one_hot(slot_row, place_row)
    below = offsets[...].astype(F32)
    index[...] = jnp.concatenate([below, below + 1.0], axis=0).T.astype(jnp.int32)
    odup[...] = jnp.concatenate([below, below], axis=0).T
    share = fractions[...]
    weight[...] = jnp.concatenate([1.0 - share, share], axis=0).T

    tab_copy.wait()
    field = own_part(latent[...], 0)
    field = field + halo_part(copies, 0, 0)
    halo_out[1] = field.astype(BF16)
    copies = start_halo(1, "y")
    started += copies
    field = own_part(field, 3) + halo_part(copies, 1, 3)
    dens = jnp.exp(along_z(field))
    density[...] = dens

    packed = dot(hot_out[...], dens.astype(BF16)).astype(BF16)
    a_out[...] = packed.reshape(a_out.shape)
    copies = swap(a_out, a_in, "x")
    started += copies
    to_y = lax.broadcasted_iota(jnp.int32, (slots, 1), 0)
    wanted = (
        (lax.rem(to_y, ncx * cap) // cap) * per_x
        + (to_y // (ncx * cap)) * cap
        + lax.rem(to_y, cap)
    ).astype(F32)
    all_slots = lax.broadcasted_iota(jnp.int32, (1, slots), 1).astype(F32)
    turn = one_hot(wanted, all_slots)
    for copy in copies:
        copy.wait_recv()
    b_out[...] = dot(turn, a_in[...].reshape(slots, depth)).astype(BF16).reshape(b_out.shape)
    copies = swap(b_out, b_in, "y")
    started += copies
    place_col = columns_of(place)
    hot_tile = jnp.concatenate(
        [one_hot(place_col, lane_of + j * LANES) for j in range(-(-slots // LANES))], axis=1
    )[:, :slots]
    for copy in copies:
        copy.wait_recv()
    block_of[...] = dot(hot_tile, b_in[...].reshape(slots, depth))

    for copy in resp_copies:
        copy.wait()
    pair_of = lax.broadcasted_iota(jnp.int32, (8, LANES), 0) // 2
    odd_row = lax.rem(lax.broadcasted_iota(jnp.int32, (8, LANES), 0), 2)
    upper = lax.broadcasted_iota(jnp.int32, (8, LANES), 1) // samples
    masks = [
        jnp.where((pair_of == j) & (odd_row == upper), 1.0, 0.0) for j in range(4)
    ]
    high_lane = lax.broadcasted_iota(jnp.int32, (8, LANES), 1) >= samples

    def forward(g, carry):
        rows = pl.ds(pl.multiple_of(g * 8, 8), 8)
        at = index[rows, :]
        near = at & (LANES - 1)
        low = jnp.take_along_axis(
            block_of[rows, 0:LANES], near, axis=1, mode="promise_in_bounds"
        )
        far = jnp.take_along_axis(
            block_of[rows, LANES : 2 * LANES], near, axis=1, mode="promise_in_bounds"
        )
        terms = jnp.where(at < LANES, low, far) * weight[rows, :]
        sample = (terms + pltpu.roll(terms, samples, 1)).astype(BF16).astype(F32)
        left = jnp.concatenate([sample * m for m in masks], axis=1).astype(BF16)
        tile_pred[rows, :] = dot(left, resp[pl.ds(pl.multiple_of(g * 512, 512), 512), :])
        return carry

    lax.fori_loop(0, tiles // 8, forward, 0, unroll=4)

    groups = observed.shape[0]
    group_row = group[...].astype(F32)
    group_of = lax.broadcasted_iota(jnp.int32, (groups, 1), 0).astype(F32)
    hot_group = one_hot(group_of, group_row)
    high, low = split(tile_pred[...])
    total = dot(hot_group, high) + dot(hot_group, low)
    predicted[...] = total
    resid = (total - observed[...]) / (sigma[...] * sigma[...])
    resid = jnp.concatenate([resid, jnp.zeros((LANES - groups, LANES), F32)], axis=0)
    hot_of_tile = one_hot(columns_of(group[...]), lane_of)
    tile_resid[...] = dot(hot_of_tile, resid.astype(BF16))

    dist = lax.broadcasted_iota(jnp.int32, (depth, 1), 0).astype(F32)
    masks2 = [jnp.concatenate([m, m], axis=0) for m in masks]

    def backward(g, carry):
        rows = pl.ds(pl.multiple_of(g * 8, 8), 8)
        back = dot_t(
            tile_resid[rows, :].astype(BF16),
            resp[pl.ds(pl.multiple_of(g * 512, 512), 512), :],
        )
        own = sum(back[:, j * LANES : (j + 1) * LANES] * masks[j] for j in range(4))
        own = own + pltpu.roll(own, samples, 1)
        parts = own * weight[rows, :]
        turned = pltpu.roll(parts, samples, 1)
        both = jnp.concatenate(
            [jnp.where(high_lane, turned, parts), jnp.where(high_lane, parts, turned)], axis=0
        )
        high = both.astype(BF16).astype(F32)
        low = both - high
        left = jnp.concatenate(
            [
                jnp.concatenate([high * m for m in masks2], axis=1).astype(BF16),
                jnp.concatenate([low * m for m in masks2], axis=1).astype(BF16),
            ],
            axis=0,
        )
        even = odup[rows, :]
        hot = []
        for j in range(4):
            at = jnp.where(high_lane[0:1], even[2 * j + 1 : 2 * j + 2], even[2 * j : 2 * j + 1])
            hot.append(one_hot(dist, at))
        out = dot_t(left, jnp.concatenate(hot, axis=1))
        lower = out[0:8] + out[16:24]
        raised = out[8:16] + out[24:32]
        tile_grad[rows, :] = lower + pltpu.roll(raised, 1, 1)
        return carry

    lax.fori_loop(0, tiles // 8, backward, 0, unroll=4)

    high, low = split(tile_grad[...])
    slot_grad = dot(hot_slot[...], high) + dot(hot_slot[...], low)

    c_out[...] = slot_grad.astype(BF16).reshape(c_out.shape)
    copies = swap(c_out, c_in, "y")
    started += copies
    wanted = (
        (lax.rem(to_y, per_x) // cap) * (ncx * cap) + (to_y // per_x) * cap + lax.rem(to_y, cap)
    ).astype(F32)
    turn = one_hot(wanted, all_slots)
    for copy in copies:
        copy.wait_recv()
    d_out[...] = dot(turn, c_in[...].reshape(slots, depth)).astype(BF16).reshape(d_out.shape)
    copies = swap(d_out, d_in, "x")
    started += copies
    for copy in copies:
        copy.wait_recv()
    dens_grad = dot(hot_back[...], d_in[...].reshape(slots, depth))

    field = density[...] * dens_grad
    halo_out[2] = field.astype(BF16)
    copies = start_halo(2, "x")
    started += copies
    field = own_part(field, 0) + halo_part(copies, 2, 0)
    halo_out[3] = field.astype(BF16)
    copies = start_halo(3, "y")
    started += copies
    field = own_part(field, 3) + halo_part(copies, 3, 3)
    gradient[...] = latent[...] + along_z(field)
    for copy in started:
        copy.wait_send()


def on_device(
    latent, observed, sigma, response, offsets, fractions, tile_group, tile_slot, send_index
):
    ncx, ncy = lax.axis_size("cx"), lax.axis_size("cy")
    rows_x, rows_y, depth = latent.shape
    tiles, samples, star_tile = response.shape
    groups = observed.shape[0] // star_tile
    cap = send_index.shape[2]
    voxels = rows_x * rows_y
    slots = ncx * ncy * cap
    tables = smoothing_tables(rows_x, rows_y, depth)
    chunks = 4
    vmem = pl.BlockSpec(memory_space=pltpu.VMEM)
    anywhere = pl.BlockSpec(memory_space=pl.ANY)
    gradient, predicted = pl.pallas_call(
        functools.partial(kernel, ncx, ncy, cap),
        out_shape=(
            jax.ShapeDtypeStruct((voxels, depth), F32),
            jax.ShapeDtypeStruct((groups, star_tile), F32),
        ),
        in_specs=[vmem, vmem, vmem, anywhere, vmem, vmem, vmem, vmem, vmem, anywhere],
        out_specs=(vmem, vmem),
        scratch_shapes=[
            pltpu.VMEM((tiles * samples, star_tile), BF16),
            pltpu.VMEM(tables.shape, BF16),
            pltpu.VMEM((4, voxels, depth), BF16),
            pltpu.VMEM((8, voxels, depth), BF16),
            pltpu.VMEM((ncx, ncy * cap, depth), BF16),
            pltpu.VMEM((ncx, ncy * cap, depth), BF16),
            pltpu.VMEM((ncy, ncx * cap, depth), BF16),
            pltpu.VMEM((ncy, ncx * cap, depth), BF16),
            pltpu.VMEM((ncy, ncx * cap, depth), BF16),
            pltpu.VMEM((ncy, ncx * cap, depth), BF16),
            pltpu.VMEM((ncx, ncy * cap, depth), BF16),
            pltpu.VMEM((ncx, ncy * cap, depth), BF16),
            pltpu.VMEM((tiles, 2 * samples), jnp.int32),
            pltpu.VMEM((tiles, 2 * samples), F32),
            pltpu.VMEM((tiles, 2 * samples), F32),
            pltpu.VMEM((tiles, depth), F32),
            pltpu.VMEM((tiles, star_tile), F32),
            pltpu.VMEM((tiles, star_tile), F32),
            pltpu.VMEM((tiles, depth), F32),
            pltpu.VMEM((slots, voxels), BF16),
            pltpu.VMEM((voxels, slots), BF16),
            pltpu.VMEM((slots, tiles), BF16),
            pltpu.VMEM((voxels, depth), F32),
            pltpu.SemaphoreType.DMA((chunks,)),
            pltpu.SemaphoreType.DMA,
            pltpu.SemaphoreType.DMA((8,)),
            pltpu.SemaphoreType.DMA((8,)),
            pltpu.SemaphoreType.DMA((2 * ncx,)),
            pltpu.SemaphoreType.DMA((2 * ncx,)),
            pltpu.SemaphoreType.DMA((2 * ncy,)),
            pltpu.SemaphoreType.DMA((2 * ncy,)),
        ],
        compiler_params=pltpu.CompilerParams(
            collective_id=0, has_side_effects=True, vmem_limit_bytes=48 * 1024 * 1024
        ),
        name="dust_map",
    )(
        latent.reshape(voxels, depth),
        observed.reshape(groups, star_tile),
        sigma.reshape(groups, star_tile),
        response.reshape(tiles * samples, star_tile),
        offsets,
        fractions,
        tile_group.reshape(1, tiles),
        tile_slot.reshape(1, tiles),
        send_index.reshape(1, slots),
        jnp.asarray(tables),
    )
    return gradient.reshape(latent.shape), predicted.reshape(-1)


def solution(mesh):
    placed = (
        P("cx", "cy", None),
        P(("cx", "cy")),
        P(("cx", "cy")),
        P(("cx", "cy"), None, None),
        P(None, ("cx", "cy")),
        P(None, ("cx", "cy")),
        P(("cx", "cy")),
        P(("cx", "cy")),
        P(("cx", "cy"), None, None),
    )
    return jax.shard_map(
        on_device,
        mesh=mesh,
        in_specs=placed,
        out_specs=(P("cx", "cy", None), P(("cx", "cy"))),
        check_vma=False,
    )
```

time: 995 us -> 83.9 us (0.08)
  other arithmetic: 488 us -> 0 us
  local copies, waits for them, and re-layouts: 409 us -> 9.18 us
  Pallas kernels: 0 us -> 72.9 us
  starting transfers between devices: 42.3 us -> 0 us
  waiting for transfers between devices: 33.3 us -> 0 us
  matrix products: 14.2 us -> 0 us
    gather x4 -> x0, local copies, waits for them, and re-layouts: 405 us -> none  [the longest x1 201 us: on_device(): lower = received[sample_at].astype(jnp.float32)]
    scatter-add x3 -> x0, other arithmetic: 350 us -> none  [the longest x1 175 us: on_device(): flat_grad = flat_grad.at[sample_at + 1].add(fractions * back)]
    add x5 -> x0, other arithmetic: 111 us -> none  [the longest x4 87.6 us: taps_over(): summed + kernel[shift_at] * lax.slice_in_dim(widened, shift_at, shift_at...]
    pallas_call x0 -> x1, Pallas kernels: none -> 72.9 us  [on_device(): pl.pallas_call(functools.partial(kernel, ncx, ncy, cap), out_shape=(jax.S...]
    ppermute x8 -> x0, starting transfers between devices: 23.2 us -> none  [the longest x4 16.1 us: padded(): lax.ppermute(tail, axis, [(i, (i + 1) % count) for i in range(ends)])]
    convert_element_type x3 -> x0, other arithmetic: 22.9 us -> none  [the longest x1 22.8 us: on_device(): columns = density.reshape(rows_x * rows_y, depth).astype(jnp.bfloat16)]
    all_to_all x2 -> x0, waiting for transfers between devices: 22.3 us -> none  [the longest x1 11.2 us: on_device(): lax.all_to_all(packed, ('cx', 'cy'), split_axis=0, concat_axis=0, tiled=T...]
    all_to_all x2 -> x0, starting transfers between devices: 19.1 us -> none  [the longest x1 14.9 us: on_device(): lax.all_to_all(packed, ('cx', 'cy'), split_axis=0, concat_axis=0, tiled=T...]
  transfers between devices with their start and end apart: 10 -> 0, of which waited for: 8 -> 0; matrix products, arithmetic and copies ran while one was open for 1% -> 0% of each run, Pallas kernels for 0% -> 0%
where the time goes in v1:
time: 83.9 us; the launch traced here: 82.7 us
  Pallas kernels  72.9 us (87%)
  local copies, waits for them, and re-layouts  9.18 us (11%)
    pallas_call x1, Pallas kernels, on_device(): pl.pallas_call(functools.partial(kernel, ncx, ncy, cap), out_shape=(jax.S...  72.9 us
    unnamed x19, local copies, waits for them, and re-layouts  9.07 us

profile of v1, /device:TPU:1, one launch (start us, length us, event | category | flops | bytes accessed | tf_op | source)
XLA Modules:
  0.0 82.7 jit_solution(138566475791901830)
XLA Ops:
  0.6 0.8 copy.13
  1.4 0.1 reshape.37.send
  1.5 0.0 copy-start
  1.5 1.5 %copy-done = bf16[14,256,256]{2,1,0:T(8,128)(2,1)S(1)} copy-done((bf16[14,256,256]{2,1,0:T(8,128)(2,1)S(1)}, bf16[14,256,256]{2,1,0:T(8,128)(2,1)}, u32[]{:S(2)}) %copy-start) | copy-done | bytes 1835032
  3.0 0.0 copy-start.1
  3.0 0.9 %copy-done.1 = f32[16,16,256]{2,1,0:T(8,128)S(1)} copy-done((f32[16,16,256]{2,1,0:T(8,128)S(1)}, f32[16,16,256]{2,1,0:T(8,128)}, u32[]{:S(2)}) %copy-start.1) | copy-done | bytes 262168
  4.0 0.0 copy-start.2
  4.0 0.9 %copy-done.2 = s32[64,512]{1,0:T(8,128)S(1)} copy-done((s32[64,512]{1,0:T(8,128)S(1)}, s32[64,512]{1,0:T(8,128)}, u32[]{:S(2)}) %copy-start.2) | copy-done | bytes 131096
  4.9 0.0 copy-start.3
  4.9 0.9 %copy-done.3 = f32[64,512]{1,0:T(8,128)S(1)} copy-done((f32[64,512]{1,0:T(8,128)S(1)}, f32[64,512]{1,0:T(8,128)}, u32[]{:S(2)}) %copy-start.3) | copy-done | bytes 131096
  5.8 0.0 copy-start.4
  5.8 0.7 copy-done.4
  6.5 0.0 copy-start.5
  6.5 0.7 copy-done.5
  7.2 0.0 copy-start.6
  7.2 0.7 copy-done.6
  7.8 0.0 copy-start.7
  7.8 0.7 copy-done.7
  8.5 72.9 %dust_map.1 = (f32[256,256]{1,0:T(8,128)S(1)}, f32[8,128]{1,0:T(8,128)S(1)}) custom-call(f32[256,256]{1,0:T(8,128)S(1)} %bitcast.8, f32[8,128]{1,0:T(8,128)S(1)} %bitcast.10, f32[8,128]{1,0:T(8,128)S(1)} %bitcast.11, bf16[32768,128]{1,0:T(8,128)(2,1)} %bitcast.15, s32[64,512]{1,0:T(8,128)S(1)} %copy-done.2, f32[64,512]{1,0:T(8,128)S(1)} %copy-done.3, ...), custom_call_target="tpu_custom_call" | custom-call | tf_op jit(solution)/shard_map/dust_map/pallas_call | solution.py:346
  81.4 0.7 copy.16
  82.1 0.6 copy.17
Async XLA Ops:
  1.5 1.5 %copy-start = (bf16[14,256,256]{2,1,0:T(8,128)(2,1)S(1)}, bf16[14,256,256]{2,1,0:T(8,128)(2,1)}, u32[]{:S(2)}) copy-start(bf16[14,256,256]{2,1,0:T(8,128)(2,1)} %constant.2.clone.tables) | copy-start | bytes 5505028
  3.0 0.9 %copy-start.1 = (f32[16,16,256]{2,1,0:T(8,128)S(1)}, f32[16,16,256]{2,1,0:T(8,128)}, u32[]{:S(2)}) copy-start(f32[16,16,256]{2,1,0:T(8,128)} %param.10) | copy-start | bytes 786436
  4.0 0.9 %copy-start.2 = (s32[64,512]{1,0:T(8,128)S(1)}, s32[64,512]{1,0:T(8,128)}, u32[]{:S(2)}) copy-start(s32[64,512]{1,0:T(8,128)} %offsets.1) | copy-start | bytes 393220
  4.9 0.9 %copy-start.3 = (f32[64,512]{1,0:T(8,128)S(1)}, f32[64,512]{1,0:T(8,128)}, u32[]{:S(2)}) copy-start(f32[64,512]{1,0:T(8,128)} %fractions.1) | copy-start | bytes 393220
  5.8 0.7 copy-start.4
  6.5 0.7 copy-start.5
  7.2 0.7 copy-start.6
  7.8 0.7 copy-start.7

commit v2 on v1

v2 whole, which is shorter than its diff:
```python
import functools

import jax
import jax.numpy as jnp
import ml_dtypes
import numpy as np
from jax import lax
from jax.experimental import pallas as pl
from jax.experimental.pallas import tpu as pltpu
from jax.sharding import PartitionSpec as P

F32, BF16 = jnp.float32, jnp.bfloat16
MESH = pl.DeviceIdType.MESH
LANES = 128
UNROLL_SENDS = 8
SET = 16
CHUNKS_X, CHUNKS_Y, CHUNKS_SWAP = (0, 1), (2, 3, 4), (5, 6, 7)


def smoothing_tables(rows_x, rows_y, depth):
    shifts = np.arange(-16, 17).astype(np.float32)
    scaled = np.sqrt(np.float32(3.0)) * np.abs(shifts) / np.float32(8.0)
    raw = (np.float32(1.0) + scaled) * np.exp(-scaled)
    taps = np.float32(0.8) * raw / np.sqrt(np.sum(raw * raw))

    def band(length, start):
        shift = np.arange(length)[None, :] + start - np.arange(length)[:, None]
        inside = np.abs(shift) <= 16
        return np.where(inside, taps[np.clip(shift + 16, 0, 32)], 0).astype(np.float32)

    whole = [np.kron(band(rows_x, s), np.eye(rows_y)) for s in (0, -rows_x, rows_x)]
    whole += [np.kron(np.eye(rows_x), band(rows_y, s)) for s in (0, -rows_y, rows_y)]
    whole += [band(depth, 0)]
    parts = []
    for table in whole:
        table = table.astype(np.float32)
        high = table.astype(ml_dtypes.bfloat16)
        parts += [high, (table - high.astype(np.float32)).astype(ml_dtypes.bfloat16)]
    return np.stack(parts)


def dot(a, b):
    return lax.dot_general(a, b, (((1,), (0,)), ((), ())), preferred_element_type=F32)


def dot_t(a, b):
    return lax.dot_general(a, b, (((1,), (1,)), ((), ())), preferred_element_type=F32)


def split(x):
    high = x.astype(BF16)
    return high, (x - high.astype(F32)).astype(BF16)


def one_hot(a, b):
    return jnp.where(a == b, 1.0, 0.0).astype(BF16)


def kernel(
    ncx, ncy, cap,
    latent_hbm, observed_hbm, sigma_hbm, response, offsets_hbm, fractions_hbm, group_hbm,
    slot_hbm, send_hbm, tables,
    gradient, predicted,
    latent, observed, sigma, offsets, fractions, group, slot, send, resp, resp_t, hot_near, tabs,
    halo_out, halo_in, there_out, there_in, back_out, back_in,
    index, weight, odup, low_index, block_of, tile_pred, tile_resid, tile_grad,
    hot_out, hot_back, hot_slot, density,
    in_sem, resp_sem, tab_sem, halo_send, halo_recv, swap_send, swap_recv, ready,
):
    cx, cy = lax.axis_index("cx"), lax.axis_index("cy")
    tiles = slot.shape[1]
    slots = ncx * ncy * cap
    samples = offsets.shape[0]
    chunk_rows = resp.shape[0] // resp_sem.shape[0]

    in_copies = [
        pltpu.make_async_copy(source, target, in_sem.at[i])
        for i, (source, target) in enumerate(
            [
                (latent_hbm, latent),
                (send_hbm, send),
                (slot_hbm, slot),
                (offsets_hbm, offsets),
                (fractions_hbm, fractions),
                (group_hbm, group),
                (observed_hbm, observed),
                (sigma_hbm, sigma),
            ]
        )
    ]
    for copy in in_copies:
        copy.start()
    tab_copy = pltpu.make_async_copy(tables, tabs, tab_sem)
    tab_copy.start()
    resp_copies = [
        pltpu.make_async_copy(
            response.at[pl.ds(i * chunk_rows, chunk_rows)],
            resp.at[pl.ds(i * chunk_rows, chunk_rows)],
            resp_sem.at[i],
        )
        for i in range(resp_sem.shape[0])
    ]
    for copy in resp_copies:
        copy.start()

    barrier = pltpu.get_barrier_semaphore()
    for k in range(1, ncx):
        pl.semaphore_signal(
            barrier, inc=1, device_id=(lax.rem(cx + k, ncx), cy), device_id_type=MESH
        )
    for k in range(1, ncy):
        pl.semaphore_signal(
            barrier, inc=1, device_id=(cx, lax.rem(cy + k, ncy)), device_id_type=MESH
        )
    in_copies[0].wait()
    halo_out[0] = latent[...].astype(BF16)
    pl.semaphore_wait(barrier, ncx + ncy - 2)
    for k in range(1, ncx):
        pl.semaphore_signal(
            ready, inc=1, device_id=(lax.rem(cx + k, ncx), cy), device_id_type=MESH
        )

    def start_halo(at, along):
        copies = []
        for side in range(2):
            step = 1 if side == 0 else -1
            if along == "x":
                to = (lax.rem(cx + step + ncx, ncx), cy)
            else:
                to = (cx, lax.rem(cy + step + ncy, ncy))
            copy = pltpu.make_async_remote_copy(
                src_ref=halo_out.at[at],
                dst_ref=halo_in.at[2 * at + side],
                send_sem=halo_send.at[2 * at + side],
                recv_sem=halo_recv.at[2 * at + side],
                device_id=to,
                device_id_type=MESH,
            )
            copy.start()
            copies.append(copy)
        return copies

    def own_part(x, at):
        high, low = split(x)
        return (
            dot(tabs[2 * at], high) + dot(tabs[2 * at + 1], high) + dot(tabs[2 * at], low)
        )

    def halo_part(copies, at, first):
        place, count = (cx, ncx) if first == 0 else (cy, ncy)
        copies[0].wait_recv()
        copies[1].wait_recv()
        left = halo_in[2 * at]
        right = halo_in[2 * at + 1]
        from_left = dot(tabs[2 * first + 2], left) + dot(tabs[2 * first + 3], left)
        from_right = dot(tabs[2 * first + 4], right) + dot(tabs[2 * first + 5], right)
        zero = jnp.zeros_like(from_left)
        return jnp.where(place > 0, from_left, zero) + jnp.where(
            place < count - 1, from_right, zero
        )

    def along_z(x):
        high, low = split(x)
        return dot(high, tabs[12]) + dot(high, tabs[13]) + dot(low, tabs[12])

    count = ncx * ncy
    me = cx * ncy + cy

    def start_swap(out, into, at):
        def send_to(k, carry):
            to = lax.rem(me + k, count)
            pltpu.make_async_remote_copy(
                src_ref=out.at[to],
                dst_ref=into.at[me],
                send_sem=swap_send.at[at],
                recv_sem=swap_recv.at[at],
                device_id=(to // ncy, lax.rem(to, ncy)),
                device_id_type=MESH,
            ).start()
            return carry

        lax.fori_loop(1, count, send_to, 0, unroll=UNROLL_SENDS)
        into[me] = out[me]

    def all_but_one(ref, sem):
        part = ref.at[pl.ds(0, count - 1)]
        return pltpu.make_async_copy(part, part, sem)

    started = []
    copies = start_halo(0, "x")
    started += copies

    for copy in in_copies[1:]:
        copy.wait()

    def columns_of(row):
        return jnp.broadcast_to(row.astype(F32), (LANES, row.shape[1])).T

    lane_of = lax.broadcasted_iota(jnp.int32, (1, LANES), 1).astype(F32)
    voxels = latent.shape[0]
    depth = latent.shape[1]
    send_col = columns_of(send[...])
    for j in range(voxels // LANES):
        hot_out[:, j * LANES : (j + 1) * LANES] = one_hot(send_col, lane_of + j * LANES)
    row_of = lax.broadcasted_iota(jnp.int32, (voxels, 1), 0).astype(F32)
    hot_back[...] = one_hot(row_of, send[...].astype(F32))
    slot_row = lax.broadcasted_iota(jnp.int32, (slots, 1), 0).astype(F32)
    hot_slot[...] = one_hot(slot_row, slot[...].astype(F32))
    below = offsets[...].astype(F32)
    index[...] = jnp.concatenate([below, below + 1.0], axis=0).T.astype(jnp.int32)
    odup[...] = jnp.concatenate([below, below], axis=0).T
    share = fractions[...]
    weight[...] = jnp.concatenate([1.0 - share, share], axis=0).T
    low_index[...] = jnp.where(below >= LANES, below - LANES, below)
    group_rows = 8 * samples

    def prepare(g, carry):
        rows = pl.ds(pl.multiple_of(g * group_rows, group_rows), group_rows)
        resp_t[g] = resp[rows, :].T
        first = g * 8
        strip = low_index[:, pl.ds(pl.multiple_of(first // LANES * LANES, LANES), LANES)]
        hots = []
        for t in range(8):
            lane = jnp.full((samples, LANES), lax.rem(first, LANES) + t, jnp.int32)
            at = jnp.take_along_axis(strip, lane, axis=1, mode="promise_in_bounds")
            hots.append(one_hot(at, lane_of))
        hot_near[rows, :] = jnp.concatenate(hots, axis=0)
        return carry

    steps = tiles // 8
    per_chunk = steps // len(resp_copies)

    def prepare_chunks(chunks):
        for i in chunks:
            resp_copies[i].wait()
            lax.fori_loop(i * per_chunk, (i + 1) * per_chunk, prepare, 0, unroll=4)


    tab_copy.wait()
    field = own_part(latent[...], 0)
    prepare_chunks(CHUNKS_X)
    field = field + halo_part(copies, 0, 0)
    halo_out[1] = field.astype(BF16)
    copies = start_halo(1, "y")
    started += copies
    field = own_part(field, 3)
    prepare_chunks(CHUNKS_Y)
    field = field + halo_part(copies, 1, 3)
    dens = jnp.exp(along_z(field))
    density[...] = dens

    packed = dot(hot_out[...], dens.astype(BF16)).astype(BF16)
    there_out[...] = packed.reshape(there_out.shape)
    pl.semaphore_wait(ready, ncx - 1)
    start_swap(there_out, there_in, 0)
    prepare_chunks(CHUNKS_SWAP)
    slot_col = columns_of(slot[...])
    hot_tile = jnp.concatenate(
        [one_hot(slot_col, lane_of + j * LANES) for j in range(-(-slots // LANES))], axis=1
    )[:, :slots]
    all_but_one(there_in, swap_recv.at[0]).wait()
    block_of[...] = dot(hot_tile, there_in[...].reshape(slots, depth))

    pair_of = lax.broadcasted_iota(jnp.int32, (8, LANES), 0) // 2
    odd_row = lax.rem(lax.broadcasted_iota(jnp.int32, (8, LANES), 0), 2)
    upper = lax.broadcasted_iota(jnp.int32, (8, LANES), 1) // samples
    keep = [(pair_of == j) & (odd_row == upper) for j in range(4)]
    masks = [jnp.where(k, 1.0, 0.0) for k in keep]
    high_lane = lax.broadcasted_iota(jnp.int32, (1, LANES), 1) >= samples
    masks = [m.astype(BF16) for m in masks]
    set_of = 8 * SET

    def forward(i, carry):
        first = pl.multiple_of(i * set_of, set_of)
        rows = pl.ds(first, set_of)
        at = index[rows, :]
        near = at & (LANES - 1)
        low = jnp.take_along_axis(
            block_of[rows, 0:LANES], near, axis=1, mode="promise_in_bounds"
        )
        far = jnp.take_along_axis(
            block_of[rows, LANES : 2 * LANES], near, axis=1, mode="promise_in_bounds"
        )
        terms = jnp.where(at < LANES, low, far) * weight[rows, :]
        sample = (terms + pltpu.roll(terms, samples, 1)).astype(BF16)
        lefts = []
        for j in range(SET):
            own = sample[8 * j : 8 * j + 8]
            lefts.append(jnp.concatenate([own * m for m in masks], axis=1))
        preds = []
        for j in range(SET):
            at_row = pl.multiple_of(first * samples + j * group_rows, group_rows)
            preds.append(dot(lefts[j], resp[pl.ds(at_row, group_rows), :]))
        tile_pred[rows, :] = jnp.concatenate(preds, axis=0)
        return carry

    lax.fori_loop(0, tiles // set_of, forward, 0)

    groups = observed.shape[0]
    group_row = group[...].astype(F32)
    group_of = lax.broadcasted_iota(jnp.int32, (groups, 1), 0).astype(F32)
    hot_group = one_hot(group_of, group_row)
    high, low = split(tile_pred[...])
    total = dot(hot_group, high) + dot(hot_group, low)
    predicted[...] = total
    resid = (total - observed[...]) / (sigma[...] * sigma[...])
    resid = jnp.concatenate([resid, jnp.zeros((LANES - groups, LANES), F32)], axis=0)
    hot_of_tile = one_hot(columns_of(group[...]), lane_of)
    tile_resid[...] = dot(hot_of_tile, resid.astype(BF16))

    masks2 = [jnp.concatenate([m, m], axis=0) for m in masks]

    def backward(i, carry):
        first = pl.multiple_of(i * set_of, set_of)
        rows = pl.ds(first, set_of)
        tr = tile_resid[rows, :].astype(BF16)
        backs = [dot(tr[8 * j : 8 * j + 8], resp_t[i * SET + j]) for j in range(SET)]
        own = jnp.concatenate(
            [
                sum(
                    jnp.where(keep[n], back[:, n * LANES : (n + 1) * LANES], 0.0)
                    for n in range(4)
                )
                for back in backs
            ],
            axis=0,
        )
        own = own + pltpu.roll(own, samples, 1)
        parts = own * weight[rows, :]
        turned = pltpu.roll(parts, samples, 1)
        v_low = jnp.where(high_lane, turned, parts)
        v_high = jnp.where(high_lane, parts, turned)
        is_far = odup[rows, :] >= LANES
        kinds = [
            jnp.where(is_far, 0.0, v_low),
            jnp.where(is_far, 0.0, v_high),
            jnp.where(is_far, v_low, 0.0),
            jnp.where(is_far, v_high, 0.0),
        ]
        lefts = []
        for j in range(SET):
            own_kinds = [kind[8 * j : 8 * j + 8] for kind in kinds]
            near = jnp.concatenate(own_kinds[0:2], axis=0).astype(BF16)
            far = jnp.concatenate(own_kinds[2:4], axis=0).astype(BF16)
            lefts.append(
                jnp.concatenate(
                    [
                        jnp.concatenate([near * m for m in masks2], axis=1),
                        jnp.concatenate([far * m for m in masks2], axis=1),
                    ],
                    axis=0,
                )
            )
        outs = []
        for j in range(SET):
            at_row = pl.multiple_of(first * samples + j * group_rows, group_rows)
            outs.append(dot(lefts[j], hot_near[pl.ds(at_row, group_rows), :]))
        lower_near = jnp.concatenate([out[0:8] for out in outs], axis=0)
        raised_near = jnp.concatenate([out[8:16] for out in outs], axis=0)
        lower_far = jnp.concatenate([out[16:24] for out in outs], axis=0)
        raised_far = jnp.concatenate([out[24:32] for out in outs], axis=0)
        raised = jnp.concatenate([raised_near, raised_far], axis=1)
        lower = jnp.concatenate([lower_near, lower_far], axis=1)
        tile_grad[rows, :] = lower + pltpu.roll(raised, 1, 1)
        return carry

    lax.fori_loop(0, tiles // set_of, backward, 0)

    high, low = split(tile_grad[...])
    slot_grad = dot(hot_slot[...], high) + dot(hot_slot[...], low)

    back_out[...] = slot_grad.astype(BF16).reshape(back_out.shape)
    start_swap(back_out, back_in, 1)
    all_but_one(back_in, swap_recv.at[1]).wait()
    dens_grad = dot(hot_back[...], back_in[...].reshape(slots, depth))

    field = density[...] * dens_grad
    halo_out[2] = field.astype(BF16)
    copies = start_halo(2, "x")
    started += copies
    field = own_part(field, 0) + halo_part(copies, 2, 0)
    halo_out[3] = field.astype(BF16)
    copies = start_halo(3, "y")
    started += copies
    field = own_part(field, 3) + halo_part(copies, 3, 3)
    gradient[...] = latent[...] + along_z(field)
    for copy in started:
        copy.wait_send()
    all_but_one(there_out, swap_send.at[0]).wait()
    all_but_one(back_out, swap_send.at[1]).wait()


def on_device(
    latent, observed, sigma, response, offsets, fractions, tile_group, tile_slot, send_index
):
    ncx, ncy = lax.axis_size("cx"), lax.axis_size("cy")
    rows_x, rows_y, depth = latent.shape
    tiles, samples, star_tile = response.shape
    groups = observed.shape[0] // star_tile
    cap = send_index.shape[2]
    voxels = rows_x * rows_y
    slots = ncx * ncy * cap
    tables = smoothing_tables(rows_x, rows_y, depth)
    chunks = 8
    vmem = pl.BlockSpec(memory_space=pltpu.VMEM)
    anywhere = pl.BlockSpec(memory_space=pltpu.HBM)
    gradient, predicted = pl.pallas_call(
        functools.partial(kernel, ncx, ncy, cap),
        out_shape=(
            jax.ShapeDtypeStruct((voxels, depth), F32),
            jax.ShapeDtypeStruct((groups, star_tile), F32),
        ),
        in_specs=[anywhere] * 10,
        out_specs=(vmem, vmem),
        scratch_shapes=[
            pltpu.VMEM((voxels, depth), F32),
            pltpu.VMEM((groups, star_tile), F32),
            pltpu.VMEM((groups, star_tile), F32),
            pltpu.VMEM((samples, tiles), jnp.int32),
            pltpu.VMEM((samples, tiles), F32),
            pltpu.VMEM((1, tiles), jnp.int32),
            pltpu.VMEM((1, tiles), jnp.int32),
            pltpu.VMEM((1, slots), jnp.int32),
            pltpu.VMEM((tiles * samples, star_tile), BF16),
            pltpu.VMEM((tiles // 8, star_tile, 8 * samples), BF16),
            pltpu.VMEM((tiles * samples, LANES), BF16),
            pltpu.VMEM(tables.shape, BF16),
            pltpu.VMEM((4, voxels, depth), BF16),
            pltpu.VMEM((8, voxels, depth), BF16),
            pltpu.VMEM((ncx * ncy, cap, depth), BF16),
            pltpu.VMEM((ncx * ncy, cap, depth), BF16),
            pltpu.VMEM((ncx * ncy, cap, depth), BF16),
            pltpu.VMEM((ncx * ncy, cap, depth), BF16),
            pltpu.VMEM((tiles, 2 * samples), jnp.int32),
            pltpu.VMEM((tiles, 2 * samples), F32),
            pltpu.VMEM((tiles, 2 * samples), F32),
            pltpu.VMEM((samples, tiles), F32),
            pltpu.VMEM((tiles, depth), F32),
            pltpu.VMEM((tiles, star_tile), F32),
            pltpu.VMEM((tiles, star_tile), F32),
            pltpu.VMEM((tiles, depth), F32),
            pltpu.VMEM((slots, voxels), BF16),
            pltpu.VMEM((voxels, slots), BF16),
            pltpu.VMEM((slots, tiles), BF16),
            pltpu.VMEM((voxels, depth), F32),
            pltpu.SemaphoreType.DMA((8,)),
            pltpu.SemaphoreType.DMA((chunks,)),
            pltpu.SemaphoreType.DMA,
            pltpu.SemaphoreType.DMA((8,)),
            pltpu.SemaphoreType.DMA((8,)),
            pltpu.SemaphoreType.DMA((2,)),
            pltpu.SemaphoreType.DMA((2,)),
            pltpu.SemaphoreType.REGULAR,
        ],
        compiler_params=pltpu.CompilerParams(
            collective_id=0, has_side_effects=True, vmem_limit_bytes=62 * 1024 * 1024
        ),
        name="dust_map",
    )(
        latent.reshape(voxels, depth),
        observed.reshape(groups, star_tile),
        sigma.reshape(groups, star_tile),
        response.reshape(tiles * samples, star_tile),
        offsets,
        fractions,
        tile_group.reshape(1, tiles),
        tile_slot.reshape(1, tiles),
        send_index.reshape(1, slots),
        jnp.asarray(tables),
    )
    return gradient.reshape(latent.shape), predicted.reshape(-1)


def solution(mesh):
    placed = (
        P("cx", "cy", None),
        P(("cx", "cy")),
        P(("cx", "cy")),
        P(("cx", "cy"), None, None),
        P(None, ("cx", "cy")),
        P(None, ("cx", "cy")),
        P(("cx", "cy")),
        P(("cx", "cy")),
        P(("cx", "cy"), None, None),
    )
    return jax.shard_map(
        on_device,
        mesh=mesh,
        in_specs=placed,
        out_specs=(P("cx", "cy", None), P(("cx", "cy"))),
        check_vma=False,
    )
```

time: 83.9 us -> 57.2 us (0.68)
  the two profiles are of different devices: /device:TPU:1 before, /device:TPU:0 now
where the time goes in v2:
time: 57.2 us; the launch traced here: 57 us
  Pallas kernels  52 us (91%)
  local copies, waits for them, and re-layouts  4.42 us (8%)
  between operations  0.64 us (1%)
    pallas_call x1, Pallas kernels, on_device(): pl.pallas_call(functools.partial(kernel, ncx, ncy, cap), out_shape=(jax.S...  52 us
    unnamed x3, local copies, waits for them, and re-layouts  3.74 us

profile of v2, /device:TPU:0, one launch (start us, length us, event | category | flops | bytes accessed | tf_op | source)
XLA Modules:
  0.0 57.0 jit_solution(15234109722876175321)
XLA Ops:
  0.6 0.8 %copy.13 = s32[1,128,4]{2,1,0:T(8,128)S(1)} copy(s32[1,128,4]{1,2,0:T(4,128)} %param.18) | data formatting | bytes 4096 | tf_op args[8]
  1.4 0.7 %reshape.37.send_hbm = s32[1,512]{1,0:T(1,128)} reshape(s32[1,128,4]{2,1,0:T(8,128)S(1)} %copy.13) | data formatting | bytes 4096 | tf_op jit(solution)/shard_map/reshape | solution.py:468
  2.1 52.0 %dust_map.1 = (f32[256,256]{1,0:T(8,128)}, f32[8,128]{1,0:T(8,128)}) custom-call(f32[256,256]{1,0:T(8,128)} %bitcast.9, f32[8,128]{1,0:T(8,128)} %bitcast.11, f32[8,128]{1,0:T(8,128)} %bitcast.12, bf16[32768,128]{1,0:T(8,128)(2,1)} %bitcast.8, s32[64,512]{1,0:T(8,128)} %offsets_hbm.1, f32[64,512]{1,0:T(8,128)} %fractions_hbm.1, s32[1,512]{1,0:T(1,128)} %bitcast.14, ...), custom_call_target="tpu_custom_call" | custom-call | tf_op jit(solution)/shard_map/dust_map/pallas_call | solution.py:407
  54.1 1.7 %copy.16 = f32[16,16,256]{2,1,0:T(8,128)} copy(f32[16,16,256]{2,1,0:T(8,128)} %bitcast.10) | data formatting | bytes 524288
  55.7 1.3 %copy.17 = f32[1024]{0:T(1024)} copy(f32[1024]{0:T(1024)} %bitcast.13) | data formatting | bytes 8192

commit v3 on v2

--- a/solution.py
+++ b/solution.py
@@ -13,7 +13,7 @@
 MESH = pl.DeviceIdType.MESH
 LANES = 128
 UNROLL_SENDS = 8
-SET = 16
+SET = 32
 CHUNKS_X, CHUNKS_Y, CHUNKS_SWAP = (0, 1), (2, 3, 4), (5, 6, 7)
 
 
@@ -64,7 +64,7 @@
     latent, observed, sigma, offsets, fractions, group, slot, send, resp, resp_t, hot_near, tabs,
     halo_out, halo_in, there_out, there_in, back_out, back_in,
     index, weight, odup, low_index, block_of, tile_pred, tile_resid, tile_grad,
-    hot_out, hot_back, hot_slot, density,
+    hot_out, hot_back, hot_slot, hot_group, hot_of_tile, density,
     in_sem, resp_sem, tab_sem, halo_send, halo_recv, swap_send, swap_recv, ready,
 ):
     cx, cy = lax.axis_index("cx"), lax.axis_index("cy")
@@ -113,7 +113,8 @@
             barrier, inc=1, device_id=(cx, lax.rem(cy + k, ncy)), device_id_type=MESH
         )
     in_copies[0].wait()
-    halo_out[0] = latent[...].astype(BF16)
+    halo_out[0] = latent[:, 0:LANES].astype(BF16)
+    halo_out[1] = latent[:, LANES:].astype(BF16)
     pl.semaphore_wait(barrier, ncx + ncy - 2)
     for k in range(1, ncx):
         pl.semaphore_signal(
@@ -141,10 +142,8 @@
         return copies
 
     def own_part(x, at):
-        high, low = split(x)
-        return (
-            dot(tabs[2 * at], high) + dot(tabs[2 * at + 1], high) + dot(tabs[2 * at], low)
-        )
+        both = dot(tabs[2 * at], jnp.concatenate(split(x), axis=1))
+        return both[:, :LANES] + both[:, LANES:] + dot(tabs[2 * at + 1], x.astype(BF16))
 
     def halo_part(copies, at, first):
         place, count = (cx, ncx) if first == 0 else (cy, ncy)
@@ -187,11 +186,30 @@
         return pltpu.make_async_copy(part, part, sem)
 
     started = []
-    copies = start_halo(0, "x")
-    started += copies
-
-    for copy in in_copies[1:]:
-        copy.wait()
+
+    def smooth(x, base, first_work, second_work):
+        low, high = x[:, :LANES], x[:, LANES:]
+        if base > 0:
+            halo_out[base] = low.astype(BF16)
+            halo_out[base + 1] = high.astype(BF16)
+        low_copies = start_halo(base, "x")
+        high_copies = start_halo(base + 1, "y")
+        started.extend(low_copies + high_copies)
+        first_work()
+        low, high = own_part(low, 0), own_part(high, 3)
+        low = low + halo_part(low_copies, base, 0)
+        halo_out[base + 2] = low.astype(BF16)
+        low_copies = start_halo(base + 2, "y")
+        high = high + halo_part(high_copies, base + 1, 3)
+        halo_out[base + 3] = high.astype(BF16)
+        high_copies = start_halo(base + 3, "x")
+        started.extend(low_copies + high_copies)
+        second_work()
+        low, high = own_part(low, 3), own_part(high, 0)
+        high = high + halo_part(high_copies, base + 3, 0)
+        low = low + halo_part(low_copies, base + 2, 3)
+        return along_z(jnp.concatenate([low, high], axis=1))
+
 
     def columns_of(row):
         return jnp.broadcast_to(row.astype(F32), (LANES, row.shape[1])).T
@@ -199,20 +217,8 @@
     lane_of = lax.broadcasted_iota(jnp.int32, (1, LANES), 1).astype(F32)
     voxels = latent.shape[0]
     depth = latent.shape[1]
-    send_col = columns_of(send[...])
-    for j in range(voxels // LANES):
-        hot_out[:, j * LANES : (j + 1) * LANES] = one_hot(send_col, lane_of + j * LANES)
-    row_of = lax.broadcasted_iota(jnp.int32, (voxels, 1), 0).astype(F32)
-    hot_back[...] = one_hot(row_of, send[...].astype(F32))
-    slot_row = lax.broadcasted_iota(jnp.int32, (slots, 1), 0).astype(F32)
-    hot_slot[...] = one_hot(slot_row, slot[...].astype(F32))
-    below = offsets[...].astype(F32)
-    index[...] = jnp.concatenate([below, below + 1.0], axis=0).T.astype(jnp.int32)
-    odup[...] = jnp.concatenate([below, below], axis=0).T
-    share = fractions[...]
-    weight[...] = jnp.concatenate([1.0 - share, share], axis=0).T
-    low_index[...] = jnp.where(below >= LANES, below - LANES, below)
     group_rows = 8 * samples
+    groups = observed.shape[0]
 
     def prepare(g, carry):
         rows = pl.ds(pl.multiple_of(g * group_rows, group_rows), group_rows)
@@ -235,18 +241,38 @@
             resp_copies[i].wait()
             lax.fori_loop(i * per_chunk, (i + 1) * per_chunk, prepare, 0, unroll=4)
 
-
-    tab_copy.wait()
-    field = own_part(latent[...], 0)
-    prepare_chunks(CHUNKS_X)
-    field = field + halo_part(copies, 0, 0)
-    halo_out[1] = field.astype(BF16)
-    copies = start_halo(1, "y")
-    started += copies
-    field = own_part(field, 3)
-    prepare_chunks(CHUNKS_Y)
-    field = field + halo_part(copies, 1, 3)
-    dens = jnp.exp(along_z(field))
+    def index_work():
+        for copy in in_copies[1:]:
+            copy.wait()
+        owner = lax.broadcasted_iota(jnp.int32, (count, 1), 0)
+        slot_lane = lax.broadcasted_iota(jnp.int32, (1, slots), 1)
+        spread = dot(
+            jnp.concatenate([send[...].astype(F32), jnp.zeros((8 - cap, count), F32)], axis=0).astype(BF16),
+            one_hot(owner, slot_lane // cap),
+        )
+        own_lane = lax.broadcasted_iota(jnp.int32, (8, 1), 0) == lax.rem(slot_lane, cap)
+        send_row = jnp.sum(jnp.where(own_lane, spread, 0.0), axis=0, keepdims=True)
+        send_col = columns_of(send_row)
+        for j in range(voxels // LANES):
+            hot_out[:, j * LANES : (j + 1) * LANES] = one_hot(send_col, lane_of + j * LANES)
+        row_of = lax.broadcasted_iota(jnp.int32, (voxels, 1), 0).astype(F32)
+        hot_back[...] = one_hot(row_of, send_row)
+        slot_row = lax.broadcasted_iota(jnp.int32, (slots, 1), 0).astype(F32)
+        hot_slot[...] = one_hot(slot_row, slot[...].astype(F32))
+        below = offsets[...].astype(F32)
+        index[...] = jnp.concatenate([below, below + 1.0], axis=0).T.astype(jnp.int32)
+        odup[...] = jnp.concatenate([below, below], axis=0).T
+        share = fractions[...]
+        weight[...] = jnp.concatenate([1.0 - share, share], axis=0).T
+        low_index[...] = jnp.where(below >= LANES, below - LANES, below)
+        group_of = lax.broadcasted_iota(jnp.int32, (groups, 1), 0).astype(F32)
+        hot_group[...] = one_hot(group_of, group[...].astype(F32))
+        hot_of_tile[...] = one_hot(columns_of(group[...]), lane_of)
+        tab_copy.wait()
+        prepare_chunks(CHUNKS_X)
+
+    field = smooth(latent[...], 0, index_work, lambda: prepare_chunks(CHUNKS_Y))
+    dens = jnp.exp(field)
     density[...] = dens
 
     packed = dot(hot_out[...], dens.astype(BF16)).astype(BF16)
@@ -296,17 +322,12 @@
 
     lax.fori_loop(0, tiles // set_of, forward, 0)
 
-    groups = observed.shape[0]
-    group_row = group[...].astype(F32)
-    group_of = lax.broadcasted_iota(jnp.int32, (groups, 1), 0).astype(F32)
-    hot_group = one_hot(group_of, group_row)
     high, low = split(tile_pred[...])
-    total = dot(hot_group, high) + dot(hot_group, low)
+    total = dot(hot_group[...], high) + dot(hot_group[...], low)
     predicted[...] = total
     resid = (total - observed[...]) / (sigma[...] * sigma[...])
     resid = jnp.concatenate([resid, jnp.zeros((LANES - groups, LANES), F32)], axis=0)
-    hot_of_tile = one_hot(columns_of(group[...]), lane_of)
-    tile_resid[...] = dot(hot_of_tile, resid.astype(BF16))
+    tile_resid[...] = dot(hot_of_tile[...], resid.astype(BF16))
 
     masks2 = [jnp.concatenate([m, m], axis=0) for m in masks]
 
@@ -375,19 +396,17 @@
     dens_grad = dot(hot_back[...], back_in[...].reshape(slots, depth))
 
     field = density[...] * dens_grad
-    halo_out[2] = field.astype(BF16)
-    copies = start_halo(2, "x")
-    started += copies
-    field = own_part(field, 0) + halo_part(copies, 2, 0)
-    halo_out[3] = field.astype(BF16)
-    copies = start_halo(3, "y")
-    started += copies
-    field = own_part(field, 3) + halo_part(copies, 3, 3)
-    gradient[...] = latent[...] + along_z(field)
+    field = smooth(field, 4, lambda: None, lambda: None)
+    gradient[...] = latent[...] + field
     for copy in started:
         copy.wait_send()
     all_but_one(there_out, swap_send.at[0]).wait()
     all_but_one(back_out, swap_send.at[1]).wait()
+
+
+def hand_out(field, stars, field_out, stars_out):
+    field_out[...] = field[...]
+    stars_out[...] = stars[...]
 
 
 def on_device(
@@ -420,13 +439,13 @@
             pltpu.VMEM((samples, tiles), F32),
             pltpu.VMEM((1, tiles), jnp.int32),
             pltpu.VMEM((1, tiles), jnp.int32),
-            pltpu.VMEM((1, slots), jnp.int32),
+            pltpu.VMEM((cap, ncx * ncy), jnp.int32),
             pltpu.VMEM((tiles * samples, star_tile), BF16),
             pltpu.VMEM((tiles // 8, star_tile, 8 * samples), BF16),
             pltpu.VMEM((tiles * samples, LANES), BF16),
             pltpu.VMEM(tables.shape, BF16),
-            pltpu.VMEM((4, voxels, depth), BF16),
-            pltpu.VMEM((8, voxels, depth), BF16),
+            pltpu.VMEM((8, voxels, depth // 2), BF16),
+            pltpu.VMEM((16, voxels, depth // 2), BF16),
             pltpu.VMEM((ncx * ncy, cap, depth), BF16),
             pltpu.VMEM((ncx * ncy, cap, depth), BF16),
             pltpu.VMEM((ncx * ncy, cap, depth), BF16),
@@ -442,12 +461,14 @@
             pltpu.VMEM((slots, voxels), BF16),
             pltpu.VMEM((voxels, slots), BF16),
             pltpu.VMEM((slots, tiles), BF16),
+            pltpu.VMEM((groups, tiles), BF16),
+            pltpu.VMEM((tiles, LANES), BF16),
             pltpu.VMEM((voxels, depth), F32),
             pltpu.SemaphoreType.DMA((8,)),
             pltpu.SemaphoreType.DMA((chunks,)),
             pltpu.SemaphoreType.DMA,
-            pltpu.SemaphoreType.DMA((8,)),
-            pltpu.SemaphoreType.DMA((8,)),
+            pltpu.SemaphoreType.DMA((16,)),
+            pltpu.SemaphoreType.DMA((16,)),
             pltpu.SemaphoreType.DMA((2,)),
             pltpu.SemaphoreType.DMA((2,)),
             pltpu.SemaphoreType.REGULAR,
@@ -465,9 +486,19 @@
         fractions,
         tile_group.reshape(1, tiles),
         tile_slot.reshape(1, tiles),
-        send_index.reshape(1, slots),
+        send_index.transpose(0, 2, 1).reshape(cap, ncx * ncy),
         jnp.asarray(tables),
     )
+    gradient, predicted = pl.pallas_call(
+        hand_out,
+        out_shape=(
+            jax.ShapeDtypeStruct((voxels, depth), F32),
+            jax.ShapeDtypeStruct((groups, star_tile), F32),
+        ),
+        in_specs=[vmem] * 2,
+        out_specs=(vmem, vmem),
+        name="hand_out",
+    )(gradient, predicted)
     return gradient.reshape(latent.shape), predicted.reshape(-1)
 
 

time: 57.2 us -> 51.4 us (0.90)
  the two profiles are of different devices: /device:TPU:0 before, /device:TPU:1 now
where the time goes in v3:
time: 51.4 us; the launch traced here: 51.3 us
  Pallas kernels  50.6 us (98%)
  between operations  0.64 us (1%)
    pallas_call x1, Pallas kernels, on_device(): pl.pallas_call(functools.partial(kernel, ncx, ncy, cap), out_shape=(jax.S...  49 us
    pallas_call x1, Pallas kernels, on_device(): pl.pallas_call(hand_out, out_shape=(jax.ShapeDtypeStruct((voxels, depth),...  1.68 us

profile of v3, /device:TPU:1, one launch (start us, length us, event | category | flops | bytes accessed | tf_op | source)
XLA Modules:
  0.0 51.3 jit_solution(8400660709656263537)
XLA Ops:
  0.6 49.0 %dust_map.1 = (f32[256,256]{1,0:T(8,128)}, f32[8,128]{1,0:T(8,128)}) custom-call(f32[256,256]{1,0:T(8,128)} %bitcast.12, f32[8,128]{1,0:T(8,128)} %bitcast.13, f32[8,128]{1,0:T(8,128)} %bitcast.14, bf16[32768,128]{1,0:T(8,128)(2,1)} %bitcast.11, s32[64,512]{1,0:T(8,128)} %offsets_hbm.1, f32[64,512]{1,0:T(8,128)} %fractions_hbm.1, s32[1,512]{1,0:T(1,128)} %bitcast.15, ...), custom_call_target="tpu_custom_call" | custom-call | tf_op jit(solution)/shard_map/dust_map/pallas_call | solution.py:426
  49.6 1.7 %hand_out.1 = (f32[256,256]{1,0:T(8,128)}, f32[8,128]{1,0:T(8,128)}) custom-call(f32[256,256]{1,0:T(8,128)} %get-tuple-element.6.field, f32[8,128]{1,0:T(8,128)} %get-tuple-element.7.stars), custom_call_target="tpu_custom_call" | custom-call | tf_op jit(solution)/shard_map/hand_out/pallas_call | solution.py:492

commit v4 on v3

--- a/solution.py
+++ b/solution.py
@@ -1,4 +1,5 @@
 import functools
+import itertools
 
 import jax
 import jax.numpy as jnp
@@ -12,7 +13,6 @@
 F32, BF16 = jnp.float32, jnp.bfloat16
 MESH = pl.DeviceIdType.MESH
 LANES = 128
-UNROLL_SENDS = 8
 SET = 32
 CHUNKS_X, CHUNKS_Y, CHUNKS_SWAP = (0, 1), (2, 3, 4), (5, 6, 7)
 
@@ -54,6 +54,17 @@
 
 def one_hot(a, b):
     return jnp.where(a == b, 1.0, 0.0).astype(BF16)
+
+
+def far_first(ring_z, ring_y, ring_x):
+    def links(step):
+        dz, dc, dy, dx = step
+        return (
+            min(dz, ring_z - dz) + min(dy, ring_y - dy) + min(dx, ring_x - dx) + 0.5 * dc
+        )
+
+    steps = itertools.product(range(ring_z), range(2), range(ring_y), range(ring_x))
+    return sorted((step for step in steps if any(step)), key=links, reverse=True)
 
 
 def kernel(
@@ -164,21 +175,23 @@
 
     count = ncx * ncy
     me = cx * ncy + cy
+    ring_x = 4 if ncy % 4 == 0 else ncy
+    ring_y, ring_z = ncy // ring_x, ncx // 2
+    at_z, at_core = cx // 2, lax.rem(cx, 2)
+    at_y, at_x = cy // ring_x, lax.rem(cy, ring_x)
 
     def start_swap(out, into, at):
-        def send_to(k, carry):
-            to = lax.rem(me + k, count)
+        for dz, dc, dy, dx in far_first(ring_z, ring_y, ring_x):
+            to_cx = lax.rem(at_z + dz, ring_z) * 2 + lax.rem(at_core + dc, 2)
+            to_cy = lax.rem(at_y + dy, ring_y) * ring_x + lax.rem(at_x + dx, ring_x)
             pltpu.make_async_remote_copy(
-                src_ref=out.at[to],
+                src_ref=out.at[to_cx * ncy + to_cy],
                 dst_ref=into.at[me],
                 send_sem=swap_send.at[at],
                 recv_sem=swap_recv.at[at],
-                device_id=(to // ncy, lax.rem(to, ncy)),
+                device_id=(to_cx, to_cy),
                 device_id_type=MESH,
             ).start()
-            return carry
-
-        lax.fori_loop(1, count, send_to, 0, unroll=UNROLL_SENDS)
         into[me] = out[me]
 
     def all_but_one(ref, sem):

time: 51.4 us -> 50.5 us (0.982)
  Pallas kernels: 50.6 us -> 49.7 us
    pallas_call x1, Pallas kernels: 49 us -> 48.1 us  [on_device(): pl.pallas_call(functools.partial(kernel, ncx, ncy, cap), out_shape=(jax.S...]
where the time goes in v4:
time: 50.5 us; the launch traced here: 50.4 us
  Pallas kernels  49.7 us (98%)
  between operations  0.64 us (1%)
    pallas_call x1, Pallas kernels, on_device(): pl.pallas_call(functools.partial(kernel, ncx, ncy, cap), out_shape=(jax.S...  48.1 us
    pallas_call x1, Pallas kernels, on_device(): pl.pallas_call(hand_out, out_shape=(jax.ShapeDtypeStruct((voxels, depth),...  1.68 us

profile of v4, /device:TPU:1, one launch (start us, length us, event | category | flops | bytes accessed | tf_op | source)
XLA Modules:
  0.0 50.4 jit_solution(10477938622655534782)
XLA Ops:
  0.6 48.1 %dust_map.1 = (f32[256,256]{1,0:T(8,128)}, f32[8,128]{1,0:T(8,128)}) custom-call(f32[256,256]{1,0:T(8,128)} %bitcast.12, f32[8,128]{1,0:T(8,128)} %bitcast.13, f32[8,128]{1,0:T(8,128)} %bitcast.14, bf16[32768,128]{1,0:T(8,128)(2,1)} %bitcast.11, s32[64,512]{1,0:T(8,128)} %offsets_hbm.1, f32[64,512]{1,0:T(8,128)} %fractions_hbm.1, s32[1,512]{1,0:T(1,128)} %bitcast.15, ...), custom_call_target="tpu_custom_call" | custom-call | tf_op jit(solution)/shard_map/dust_map/pallas_call | solution.py:439
  48.7 1.7 %hand_out.1 = (f32[256,256]{1,0:T(8,128)}, f32[8,128]{1,0:T(8,128)}) custom-call(f32[256,256]{1,0:T(8,128)} %get-tuple-element.6.field, f32[8,128]{1,0:T(8,128)} %get-tuple-element.7.stars), custom_call_target="tpu_custom_call" | custom-call | tf_op jit(solution)/shard_map/hand_out/pallas_call | solution.py:505

commit v5 on v4

--- a/solution.py
+++ b/solution.py
@@ -13,8 +13,8 @@
 F32, BF16 = jnp.float32, jnp.bfloat16
 MESH = pl.DeviceIdType.MESH
 LANES = 128
-SET = 32
-CHUNKS_X, CHUNKS_Y, CHUNKS_SWAP = (0, 1), (2, 3, 4), (5, 6, 7)
+SET = 64
+CHUNKS_X, CHUNKS_Y, CHUNKS_SWAP = tuple(range(2)), tuple(range(2, 6)), tuple(range(6, 16))
 
 
 def smoothing_tables(rows_x, rows_y, depth):
@@ -433,7 +433,7 @@
     voxels = rows_x * rows_y
     slots = ncx * ncy * cap
     tables = smoothing_tables(rows_x, rows_y, depth)
-    chunks = 8
+    chunks = 16
     vmem = pl.BlockSpec(memory_space=pltpu.VMEM)
     anywhere = pl.BlockSpec(memory_space=pltpu.HBM)
     gradient, predicted = pl.pallas_call(

time: 50.5 us -> 49.3 us (0.976)
  Pallas kernels: 49.7 us -> 48.6 us
    pallas_call x1, Pallas kernels: 48.1 us -> 46.9 us  [on_device(): pl.pallas_call(functools.partial(kernel, ncx, ncy, cap), out_shape=(jax.S...]
where the time goes in v5:
time: 49.3 us; the launch traced here: 49.2 us
  Pallas kernels  48.6 us (99%)
  between operations  0.64 us (1%)
    pallas_call x1, Pallas kernels, on_device(): pl.pallas_call(functools.partial(kernel, ncx, ncy, cap), out_shape=(jax.S...  46.9 us
    pallas_call x1, Pallas kernels, on_device(): pl.pallas_call(hand_out, out_shape=(jax.ShapeDtypeStruct((voxels, depth),...  1.68 us

profile of v5, /device:TPU:1, one launch (start us, length us, event | category | flops | bytes accessed | tf_op | source)
XLA Modules:
  0.0 49.2 jit_solution(15081771387400343122)
XLA Ops:
  0.6 46.9 %dust_map.1 = (f32[256,256]{1,0:T(8,128)}, f32[8,128]{1,0:T(8,128)}) custom-call(f32[256,256]{1,0:T(8,128)} %bitcast.12, f32[8,128]{1,0:T(8,128)} %bitcast.13, f32[8,128]{1,0:T(8,128)} %bitcast.14, bf16[32768,128]{1,0:T(8,128)(2,1)} %bitcast.11, s32[64,512]{1,0:T(8,128)} %offsets_hbm.1, f32[64,512]{1,0:T(8,128)} %fractions_hbm.1, s32[1,512]{1,0:T(1,128)} %bitcast.15, ...), custom_call_target="tpu_custom_call" | custom-call | tf_op jit(solution)/shard_map/dust_map/pallas_call | solution.py:439
  47.5 1.7 %hand_out.1 = (f32[256,256]{1,0:T(8,128)}, f32[8,128]{1,0:T(8,128)}) custom-call(f32[256,256]{1,0:T(8,128)} %get-tuple-element.6.field, f32[8,128]{1,0:T(8,128)} %get-tuple-element.7.stars), custom_call_target="tpu_custom_call" | custom-call | tf_op jit(solution)/shard_map/hand_out/pallas_call | solution.py:505

commit v6 on v5

--- a/solution.py
+++ b/solution.py
@@ -99,7 +99,17 @@
             ]
         )
     ]
-    for copy in in_copies:
+    in_copies[0].start()
+    barrier = pltpu.get_barrier_semaphore()
+    for k in range(1, ncx):
+        pl.semaphore_signal(
+            barrier, inc=1, device_id=(lax.rem(cx + k, ncx), cy), device_id_type=MESH
+        )
+    for k in range(1, ncy):
+        pl.semaphore_signal(
+            barrier, inc=1, device_id=(cx, lax.rem(cy + k, ncy)), device_id_type=MESH
+        )
+    for copy in in_copies[1:]:
         copy.start()
     tab_copy = pltpu.make_async_copy(tables, tabs, tab_sem)
     tab_copy.start()
@@ -114,23 +124,10 @@
     for copy in resp_copies:
         copy.start()
 
-    barrier = pltpu.get_barrier_semaphore()
-    for k in range(1, ncx):
-        pl.semaphore_signal(
-            barrier, inc=1, device_id=(lax.rem(cx + k, ncx), cy), device_id_type=MESH
-        )
-    for k in range(1, ncy):
-        pl.semaphore_signal(
-            barrier, inc=1, device_id=(cx, lax.rem(cy + k, ncy)), device_id_type=MESH
-        )
     in_copies[0].wait()
     halo_out[0] = latent[:, 0:LANES].astype(BF16)
     halo_out[1] = latent[:, LANES:].astype(BF16)
     pl.semaphore_wait(barrier, ncx + ncy - 2)
-    for k in range(1, ncx):
-        pl.semaphore_signal(
-            ready, inc=1, device_id=(lax.rem(cx + k, ncx), cy), device_id_type=MESH
-        )
 
     def start_halo(at, along):
         copies = []
@@ -205,8 +202,8 @@
         if base > 0:
             halo_out[base] = low.astype(BF16)
             halo_out[base + 1] = high.astype(BF16)
+        high_copies = start_halo(base + 1, "y")
         low_copies = start_halo(base, "x")
-        high_copies = start_halo(base + 1, "y")
         started.extend(low_copies + high_copies)
         first_work()
         low, high = own_part(low, 0), own_part(high, 3)
@@ -255,6 +252,10 @@
             lax.fori_loop(i * per_chunk, (i + 1) * per_chunk, prepare, 0, unroll=4)
 
     def index_work():
+        for k in range(1, ncx):
+            pl.semaphore_signal(
+                ready, inc=1, device_id=(lax.rem(cx + k, ncx), cy), device_id_type=MESH
+            )
         for copy in in_copies[1:]:
             copy.wait()
         owner = lax.broadcasted_iota(jnp.int32, (count, 1), 0)

time: 49.3 us -> 49.3 us (level)
  no operation moved by 1% of the time
where the time goes in v6:
time: 49.3 us; the launch traced here: 49.2 us
  Pallas kernels  48.6 us (99%)
  between operations  0.64 us (1%)
    pallas_call x1, Pallas kernels, on_device(): pl.pallas_call(functools.partial(kernel, ncx, ncy, cap), out_shape=(jax.S...  46.9 us
    pallas_call x1, Pallas kernels, on_device(): pl.pallas_call(hand_out, out_shape=(jax.ShapeDtypeStruct((voxels, depth),...  1.68 us

profile of v6, /device:TPU:1, one launch (start us, length us, event | category | flops | bytes accessed | tf_op | source)
XLA Modules:
  0.0 49.2 jit_solution(15803866475694305899)
XLA Ops:
  0.6 46.9 %dust_map.1 = (f32[256,256]{1,0:T(8,128)}, f32[8,128]{1,0:T(8,128)}) custom-call(f32[256,256]{1,0:T(8,128)} %bitcast.12, f32[8,128]{1,0:T(8,128)} %bitcast.13, f32[8,128]{1,0:T(8,128)} %bitcast.14, bf16[32768,128]{1,0:T(8,128)(2,1)} %bitcast.11, s32[64,512]{1,0:T(8,128)} %offsets_hbm.1, f32[64,512]{1,0:T(8,128)} %fractions_hbm.1, s32[1,512]{1,0:T(1,128)} %bitcast.15, ...), custom_call_target="tpu_custom_call" | custom-call | tf_op jit(solution)/shard_map/dust_map/pallas_call | solution.py:440
  47.5 1.7 %hand_out.1 = (f32[256,256]{1,0:T(8,128)}, f32[8,128]{1,0:T(8,128)}) custom-call(f32[256,256]{1,0:T(8,128)} %get-tuple-element.6.field, f32[8,128]{1,0:T(8,128)} %get-tuple-element.7.stars), custom_call_target="tpu_custom_call" | custom-call | tf_op jit(solution)/shard_map/hand_out/pallas_call | solution.py:506
